TPU v7x, 256 devices: a whole 4x4x8 slice. The times are simulated.
256 devices in a mesh: dp: 16 (over z_lo, x, core), expert: 16 (over z_hi, y).
Axes of the slice: x: 4, y: 4, z: 8 (z_hi: 4, z_lo: 2; z = z_hi * 2 + z_lo), core: 2. Of those that a mesh axis runs over, the one named last changes fastest.
Arguments:
- tokens: bfloat16 [32768, 3584], P(('dp', 'expert')), may hold values from -6 to 6
- out_grad: bfloat16 [32768, 3584], P(('dp', 'expert')), may hold values from -6 to 6
- routes: int32 [32768, 2], P(('dp', 'expert')), may hold values from 0 to 15, all different within a row; in each aligned block of 128 rows (0 to 127, 128 to 255, ...) at most 20 rows name the same one
- probs: bfloat16 [32768, 2], P(('dp', 'expert')), may hold values from 0.099609375 to 1
- swap_flags: int32 [16], replicated, may hold values from 0 to 1, as said below
- up_weight: bfloat16 [16, 1024, 3584], P('expert', 'dp'), may hold values from -4 to 4
- down_weight: bfloat16 [16, 1024, 3584], P('expert', 'dp'), may hold values from -4 to 4
- up_first: float32 [16, 1024, 3584], P('expert', 'dp'), may hold values from -3 to 3
- up_second: float32 [16, 1024, 3584], P('expert', 'dp'), may hold values from 0.02 to 0.3
- down_first: float32 [16, 1024, 3584], P('expert', 'dp'), may hold values from -3 to 3
- down_second: float32 [16, 1024, 3584], P('expert', 'dp'), may hold values from 0.02 to 0.3
Outputs:
- token_grad: bfloat16 [32768, 3584], P(('dp', 'expert'))
- new_up_weight: bfloat16 [16, 1024, 3584], P('expert', 'dp')
- new_down_weight: bfloat16 [16, 1024, 3584], P('expert', 'dp')
- new_up_first: float32 [16, 1024, 3584], P('expert', 'dp')
- new_up_second: float32 [16, 1024, 3584], P('expert', 'dp')
- new_down_first: float32 [16, 1024, 3584], P('expert', 'dp')
- new_down_second: float32 [16, 1024, 3584], P('expert', 'dp')
Inputs may be any that keep to these rules, and one draw needn't show every extreme that they name: `routes`: each row names 2 different experts. Within the 128 rows of one device no expert is named by more than 20 rows, a bound that some block reaches. swap_flags[s] equals swap_flags[s XOR (8)]; the slots 16 // 2 - 1 and 15 always trade places.
All inputs are finite; a program needn't handle non-finite values.
Results may differ from a plain program's by a relative error of at most 0.022.
Values may be sent and summed in bfloat16 or wider, within the bound.
No kernel may reach another device: no remote copies, remote signals or barrier semaphores. Data moves between devices by JAX's collectives and lax.ppermute only.
A program may use at most 128 MiB of HBM per device.

v0:
```python
import jax
import jax.numpy as jnp
from jax import lax
from jax.sharding import PartitionSpec as P

ADAM_STEP = 20


beta_first = 0.9
beta_second = 0.95
step_size = 0.05
adam_epsilon = 1e-08


def partner_2(shard, axis, stride):
    return lax.ppermute(shard, axis, [(i, i ^ 1 << stride) for i in range(lax.axis_size(axis))])


def adam_update(weight, first, second, gradient):
    first_new = beta_first * first + (1.0 - beta_first) * gradient
    second_new = beta_second * second + (1.0 - beta_second) * gradient * gradient
    corr_first = 1.0 - beta_first**ADAM_STEP
    corr_second = 1.0 - beta_second**ADAM_STEP
    stepped = weight.astype(jnp.float32) - step_size * (first_new / corr_first) / (
        jnp.sqrt(second_new / corr_second) + adam_epsilon
    )
    return (stepped.astype(jnp.bfloat16), first_new, second_new)


def on_device(
    tokens,
    out_grad,
    routes,
    probs,
    swap_flags,
    up_weight,
    down_weight,
    up_first,
    up_second,
    down_first,
    down_second,
):
    model_width = tokens.shape[1]
    tok_rows, top_count = routes.shape
    experts = lax.axis_size("expert")
    half_axis = experts // 2
    swap_bit = half_axis.bit_length() - 1
    capacity = max(2, tok_rows * top_count * 5 // (4 * experts))
    buffer_rows = experts * capacity
    hidden_units = up_weight.shape[1] * lax.axis_size("dp")
    inv_model = model_width ** (-0.5)
    inv_hidden = hidden_units ** (-0.5)
    contract_last = (((1,), (1,)), ((), ()))
    contract_first = (((0,), (0,)), ((), ()))
    my_index = lax.axis_index("expert")
    expert_ids = jnp.arange(experts, dtype=jnp.int32)
    flag_mine = jnp.sum(jnp.where(expert_ids == my_index, swap_flags, 0))
    new_slot = jnp.where(swap_flags == 1, jnp.bitwise_xor(expert_ids, half_axis), expert_ids)
    weights = (up_weight[0], down_weight[0])
    moments = (up_first[0], up_second[0], down_first[0], down_second[0])
    partner_weights = partner_2((weights[0], weights[1]), "expert", swap_bit)
    partner_moments = (
        partner_2(moments[0].astype(jnp.bfloat16), "expert", swap_bit).astype(jnp.float32),
        partner_2(moments[1].astype(jnp.bfloat16), "expert", swap_bit).astype(jnp.float32),
        partner_2(moments[2].astype(jnp.bfloat16), "expert", swap_bit).astype(jnp.float32),
        partner_2(moments[3].astype(jnp.bfloat16), "expert", swap_bit).astype(jnp.float32),
    )
    swapped = flag_mine == 1

    def choose_one(current, partner):
        return jnp.where(swapped, partner, current)

    weights, moments = (
        jax.tree.map(choose_one, weights, partner_weights),
        jax.tree.map(choose_one, moments, partner_moments),
    )
    destination = jnp.sum(
        jnp.where(routes[:, :, None] == expert_ids[None, None, :], new_slot[None, None, :], 0),
        axis=2,
    )
    pair_dest = destination.reshape(-1)
    dest_onehot = (pair_dest[:, None] == expert_ids[None, :]).astype(jnp.int32)
    earlier = jnp.cumsum(dest_onehot, axis=0) - dest_onehot
    position = jnp.sum(earlier * dest_onehot, axis=1)
    buffer_index = pair_dest * capacity + position
    buffer_ids = jnp.arange(buffer_rows, dtype=jnp.int32)
    pair_select = (buffer_ids[:, None] == buffer_index[None, :]).astype(jnp.bfloat16)
    token_select = jnp.sum(pair_select.reshape(buffer_rows, tok_rows, top_count), axis=2)
    send_tokens = (
        jnp.dot(token_select, tokens, preferred_element_type=jnp.float32)
        .astype(jnp.bfloat16)
        .reshape(experts, capacity, model_width)
    )
    send_cotan = (
        jnp.dot(token_select, out_grad, preferred_element_type=jnp.float32)
        .astype(jnp.bfloat16)
        .reshape(experts, capacity, model_width)
    )
    send_probs = (
        jnp.dot(pair_select, probs.reshape(-1), preferred_element_type=jnp.float32)
        .astype(jnp.bfloat16)
        .reshape(experts, capacity)
    )
    got_tokens, got_cotan, got_probs = (
        lax.all_to_all(send_tokens, "expert", split_axis=0, concat_axis=0, tiled=True),
        lax.all_to_all(send_cotan, "expert", split_axis=0, concat_axis=0, tiled=True),
        lax.all_to_all(send_probs, "expert", split_axis=0, concat_axis=0, tiled=True),
    )
    expert_rows = got_tokens.reshape(buffer_rows, model_width)
    cotan_rows = got_cotan.reshape(buffer_rows, model_width)
    row_probs = got_probs.reshape(buffer_rows).astype(jnp.float32)
    up_local, down_local = weights
    up_full, down_full = (
        lax.all_gather(up_local, "dp", axis=0, tiled=True),
        lax.all_gather(down_local, "dp", axis=0, tiled=True),
    )
    pre_act = (
        lax.dot_general(expert_rows, up_full, contract_last, preferred_element_type=jnp.float32)
        * inv_model
    )
    back_proj = lax.dot_general(
        cotan_rows, down_full, contract_last, preferred_element_type=jnp.float32
    )
    sigmoid_act = jax.nn.sigmoid(pre_act)
    activ = (pre_act * sigmoid_act).astype(jnp.bfloat16)
    delta = (
        row_probs[:, None]
        * back_proj
        * inv_hidden
        * sigmoid_act
        * (1.0 + pre_act * (1.0 - sigmoid_act))
    ).astype(jnp.bfloat16)
    scaled = (row_probs[:, None] * cotan_rows.astype(jnp.float32)).astype(jnp.bfloat16)
    pair_grad = jnp.dot(delta, up_full, preferred_element_type=jnp.float32) * inv_model
    returned = lax.all_to_all(
        pair_grad.astype(jnp.bfloat16).reshape(experts, capacity, model_width),
        "expert",
        split_axis=0,
        concat_axis=0,
        tiled=True,
    )
    token_grad = lax.dot_general(
        token_select,
        returned.reshape(buffer_rows, model_width),
        contract_first,
        preferred_element_type=jnp.float32,
    ).astype(jnp.bfloat16)
    up_part = (
        lax.dot_general(delta, expert_rows, contract_first, preferred_element_type=jnp.float32)
        * inv_model
    )
    down_part = (
        lax.dot_general(activ, scaled, contract_first, preferred_element_type=jnp.float32)
        * inv_hidden
    )
    summed = lax.psum_scatter(
        jnp.stack((up_part, down_part), axis=1).astype(jnp.bfloat16),
        "dp",
        scatter_dimension=0,
        tiled=True,
    ).astype(jnp.float32)
    up_moment_one, up_moment_two, down_moment_one, down_moment_two = moments
    new_up, up_first_new, up_second_new = adam_update(
        up_local, up_moment_one, up_moment_two, summed[:, 0]
    )
    new_down, down_first_new, down_second_new = adam_update(
        down_local, down_moment_one, down_moment_two, summed[:, 1]
    )
    weights_out = (new_up, new_down)
    moments_out = (up_first_new, up_second_new, down_first_new, down_second_new)
    return (
        token_grad,
        weights_out[0][None],
        weights_out[1][None],
        moments_out[0][None],
        moments_out[1][None],
        moments_out[2][None],
        moments_out[3][None],
    )


def solution(mesh):
    in_specs = (
        P(("dp", "expert"), None),
        P(("dp", "expert"), None),
        P(("dp", "expert"), None),
        P(("dp", "expert"), None),
        P(),
        P("expert", "dp", None),
        P("expert", "dp", None),
        P("expert", "dp", None),
        P("expert", "dp", None),
        P("expert", "dp", None),
        P("expert", "dp", None),
    )
    out_specs = (
        P(("dp", "expert"), None),
        P("expert", "dp", None),
        P("expert", "dp", None),
        P("expert", "dp", None),
        P("expert", "dp", None),
        P("expert", "dp", None),
        P("expert", "dp", None),
    )
    return jax.shard_map(
        on_device, mesh=mesh, in_specs=in_specs, out_specs=out_specs, check_vma=False
    )
```

profile of v0, /device:TPU:8, one launch (start us, length us, event | category | flops | bytes accessed | tf_op | source)
XLA Modules:
  0.0 523.0 jit_solution(14422215837059954153)
XLA Ops:
  7.2 7.3 %collective-permute-start.1 = (bf16[64,3584]{1,0:T(8,128)(2,1)}, bf16[64,3584]{1,0:T(8,128)(2,1)S(1)}, u32[]{:S(2)}, u32[]{:S(2)}) collective-permute-start(bf16[64,3584]{1,0:T(8,128)(2,1)} %bitcast.126), channel_id=1, source_target_pairs={{0,8},{1,9},{2,10},{3,11},{4,12},{5,13},{6,14},{7,15},{8,0},{9,1},... | collective-permute-start | bytes 1376264 | tf_op jit(solution)/shard_map/ppermute | solution.py:16
  16.5 11.0 %collective-permute-done.1 = bf16[64,3584]{1,0:T(8,128)(2,1)S(1)} collective-permute-done((bf16[64,3584]{1,0:T(8,128)(2,1)}, bf16[64,3584]{1,0:T(8,128)(2,1)S(1)}, u32[]{:S(2)}, u32[]{:S(2)}) %collective-permute-start.1) | collective-permute-done | bytes 458784 | tf_op jit(solution)/shard_map/ppermute | solution.py:16
  27.5 1.8 broadcast_select_fusion
  29.4 12.7 %collective-permute-start = (bf16[64,3584]{1,0:T(8,128)(2,1)}, bf16[64,3584]{1,0:T(8,128)(2,1)S(1)}, u32[]{:S(2)}, u32[]{:S(2)}) collective-permute-start(bf16[64,3584]{1,0:T(8,128)(2,1)} %bitcast.127), channel_id=1, source_target_pairs={{0,8},{1,9},{2,10},{3,11},{4,12},{5,13},{6,14},{7,15},{8,0},{9,1},... | collective-permute-start | bytes 1376264 | tf_op jit(solution)/shard_map/ppermute | solution.py:16
  42.1 14.9 %collective-permute-done = bf16[64,3584]{1,0:T(8,128)(2,1)S(1)} collective-permute-done((bf16[64,3584]{1,0:T(8,128)(2,1)}, bf16[64,3584]{1,0:T(8,128)(2,1)S(1)}, u32[]{:S(2)}, u32[]{:S(2)}) %collective-permute-start) | collective-permute-done | bytes 458784 | tf_op jit(solution)/shard_map/ppermute | solution.py:16
  61.5 16.6 %all-to-all-start = ((bf16[16,1,20]{2,1,0:T(2,128)(2,1)}), bf16[16,1,20]{2,1,0:T(2,128)(2,1)S(1)}, u32[]{:S(2)}, u32[]{:S(2)}) async-start(bf16[16,1,20]{2,1,0:T(2,128)(2,1)} %all_to_all.20), calls=%async_computation | async-start | bytes 16384 | tf_op jit(solution)/shard_map/all_to_all | solution.py:107
  79.2 2.2 reshape.88
  81.4 5.3 %all-to-all-done = bf16[16,1,20]{2,1,0:T(2,128)(2,1)S(1)} async-done(((bf16[16,1,20]{2,1,0:T(2,128)(2,1)}), bf16[16,1,20]{2,1,0:T(2,128)(2,1)S(1)}, u32[]{:S(2)}, u32[]{:S(2)}) %all-to-all-start) | async-done | bytes 672 | tf_op jit(solution)/shard_map/all_to_all | solution.py:107
  86.6 5.7 %all-to-all-start.1 = ((bf16[16,20,3584]{2,1,0:T(8,128)(2,1)}), bf16[16,20,3584]{2,1,0:T(8,128)(2,1)}, u32[]{:S(2)}, u32[]{:S(2)}) async-start(bf16[16,20,3584]{2,1,0:T(8,128)(2,1)} %reshape.88), calls=%async_computation.1 | async-start | bytes 5505024 | tf_op jit(solution)/shard_map/all_to_all | solution.py:106
  93.1 2.3 reshape.90
  95.3 76.4 %all-to-all-done.1 = bf16[16,20,3584]{2,1,0:T(8,128)(2,1)} async-done(((bf16[16,20,3584]{2,1,0:T(8,128)(2,1)}), bf16[16,20,3584]{2,1,0:T(8,128)(2,1)}, u32[]{:S(2)}, u32[]{:S(2)}) %all-to-all-start.1) | async-done | bytes 2293792 | tf_op jit(solution)/shard_map/all_to_all | solution.py:106
  171.8 5.0 all-to-all-start.2
  177.1 4.1 reshape.89
  181.2 69.8 %all-to-all-done.2 = bf16[16,20,3584]{2,1,0:T(8,128)(2,1)S(1)} async-done(((bf16[16,20,3584]{2,1,0:T(8,128)(2,1)}), bf16[16,20,3584]{2,1,0:T(8,128)(2,1)S(1)}, u32[]{:S(2)}, u32[]{:S(2)}) %all-to-all-start.2) | async-done | bytes 2293792 | tf_op jit(solution)/shard_map/all_to_all | solution.py:105
  251.0 2.1 reshape.91
  253.1 6.5 %convolution_multiply_fusion.1 = f32[320,1024]{1,0:T(8,128)S(1)} fusion(bf16[320,3584]{1,0:T(8,128)(2,1)} %reshape.91, bf16[1024,3584]{1,0:T(8,128)(2,1)} %all-gather.5.cloned.1.call-done), kind=kOutput, calls=%fused_computation.12 | convolution fusion | flops 2349137920 | bytes 10944512 | tf_op jit(solution)/shard_map/dot_general | solution.py:118
  260.8 6.4 %fusion.1 = bf16[1024,1,3584]{2,0,1:T(8,128)(2,1)} fusion(bf16[320,3584]{1,0:T(8,128)(2,1)S(1)} %copy-done.11, f32[320]{0:T(512)S(1)} %reshape.94, f32[320,1024]{1,0:T(8,128)S(1)} %convolution_multiply_fusion.1), kind=kOutput, calls=%fused_computation.4 | convolution fusion | flops 2361229312 | bytes 10945792 | tf_op jit(solution)/shard_map/dot_general | solution.py:153
  267.2 6.3 %fusion.7 = bf16[320,1024]{1,0:T(8,128)(2,1)S(1)} fusion(bf16[320,3584]{1,0:T(8,128)(2,1)S(1)} %copy-done.11, bf16[1024,3584]{1,0:T(8,128)(2,1)} %all-gather.3.cloned.1.call-done, f32[320,1024]{1,0:T(8,128)} %copy-done.18, f32[320]{0:T(512)S(1)} %reshape.94), kind=kOutput, calls=%fused_computation.19 | convolution fusion | flops 2352414720 | bytes 11601152 | tf_op jit(solution)/shard_map/dot_general | solution.py:121
  273.5 4.3 fusion
  277.8 6.5 %pad_maximum_fusion = bf16[1024,2,3584]{2,0,1:T(8,128)(2,1)} fusion(bf16[1024,1,3584]{2,0,1:T(8,128)(2,1)S(1)} %copy-done.2, bf16[1024,1,3584]{2,0,1:T(8,128)(2,1)S(1)} %fusion), kind=kLoop, calls=%fused_computation | loop fusion | flops 7340032 | bytes 29360128 | tf_op jit(solution)/shard_map/stack | solution.py:157
  285.4 5.6 %fusion.2 = bf16[320,3584]{1,0:T(8,128)(2,1)S(1)} fusion(bf16[320,1024]{1,0:T(8,128)(2,1)S(1)} %copy-done.17, bf16[1024,3584]{1,0:T(8,128)(2,1)} %all-gather.5.cloned.1.call-done), kind=kOutput, calls=%fused_computation.6 | convolution fusion | flops 2351104000 | bytes 10289152 | tf_op jit(solution)/shard_map/dot_general | solution.py:134
  291.0 2.2 reshape.92
  293.2 5.0 all-to-all-start.3
  298.3 2.1 bitcast_convert_fusion
  300.4 5.4 %collective-permute-start.5 = (bf16[64,3584]{1,0:T(8,128)(2,1)}, bf16[64,3584]{1,0:T(8,128)(2,1)S(1)}, u32[]{:S(2)}, u32[]{:S(2)}) collective-permute-start(bf16[64,3584]{1,0:T(8,128)(2,1)} %bitcast_convert_fusion), channel_id=1, source_target_pairs={{0,8},{1,9},{2,10},{3,11},{4,12},{5,13},{6,14},{7,15},{8,0},{9,1},... | collective-permute-start | bytes 1376264 | tf_op jit(solution)/shard_map/ppermute | solution.py:16
  305.8 2.0 bitcast_convert_fusion.1
  309.1 5.4 %collective-permute-start.2 = (bf16[64,3584]{1,0:T(8,128)(2,1)}, bf16[64,3584]{1,0:T(8,128)(2,1)}, u32[]{:S(2)}, u32[]{:S(2)}) collective-permute-start(bf16[64,3584]{1,0:T(8,128)(2,1)} %bitcast_convert_fusion.3), channel_id=1, source_target_pairs={{0,8},{1,9},{2,10},{3,11},{4,12},{5,13},{6,14},{7,15},{8,0},{9,1},... | collective-permute-start | bytes 1376264 | tf_op jit(solution)/shard_map/ppermute | solution.py:16
  315.9 64.7 %all-to-all-done.3 = bf16[16,20,3584]{2,1,0:T(8,128)(2,1)S(1)} async-done(((bf16[16,20,3584]{2,1,0:T(8,128)(2,1)}), bf16[16,20,3584]{2,1,0:T(8,128)(2,1)S(1)}, u32[]{:S(2)}, u32[]{:S(2)}) %all-to-all-start.3) | async-done | bytes 2293792 | tf_op jit(solution)/shard_map/all_to_all | solution.py:135
  380.5 2.1 reshape.93
  382.6 3.4 convolution_convert_fusion.2
  386.0 124.2 %reduce-scatter.2.cloned.1.call-done = bf16[64,2,3584]{2,0,1:T(8,128)(2,1)} async-done(((bf16[1024,2,3584]{2,0,1:T(8,128)(2,1)}), bf16[64,2,3584]{2,0,1:T(8,128)(2,1)}) %reduce-scatter.2.cloned.1.call-update) | async-done | bytes 917520 | tf_op jit(solution)/shard_map/reduce_scatter | solution.py:156
  512.2 4.3 fusion.30
  (80 shorter events, 14.9 us)
Async XLA Ops:
  7.2 71.2 %copy-start = (bf16[128,3584]{1,0:T(8,128)(2,1)S(1)}, bf16[128,3584]{1,0:T(8,128)(2,1)}, u32[]{:S(2)}) copy-start(bf16[128,3584]{1,0:T(8,128)(2,1)} %param.12) | copy-start | bytes 2752516
  7.2 51.7 %copy-start.14 = (s32[128,2]{0,1:T(2,128)S(1)}, s32[128,2]{0,1:T(2,128)}, u32[]{:S(2)}) copy-start(s32[128,2]{0,1:T(2,128)} %param.13) | copy-start | bytes 3076
  7.2 53.0 %copy-start.15 = (bf16[128,2]{0,1:T(2,128)(2,1)S(1)}, bf16[128,2]{0,1:T(2,128)(2,1)}, u32[]{:S(2)}) copy-start(bf16[128,2]{0,1:T(2,128)(2,1)} %param.14) | copy-start | bytes 1540
  7.2 245.9 %all-gather.5.cloned.1.call-start = ((), (), s32[]{:S(2)}) async-start(), calls=%async_computation.6 | async-start | bytes 7798784 | tf_op jit(solution)/shard_map/all_gather | solution.py:114
  7.2 20.3 %collective-permute-start.1 = (bf16[64,3584]{1,0:T(8,128)(2,1)}, bf16[64,3584]{1,0:T(8,128)(2,1)S(1)}, u32[]{:S(2)}, u32[]{:S(2)}) collective-permute-start(bf16[64,3584]{1,0:T(8,128)(2,1)} %bitcast.126), channel_id=1, source_target_pairs={{0,8},{1,9},{2,10},{3,11},{4,12},{5,13},{6,14},{7,15},{8,0},{9,1},... | collective-permute-start | bytes 1376264 | tf_op jit(solution)/shard_map/ppermute | solution.py:16
  29.4 237.8 %all-gather.3.cloned.1.call-start = ((), (), s32[]{:S(2)}) async-start(), calls=%async_computation.5 | async-start | bytes 7798784 | tf_op jit(solution)/shard_map/all_gather | solution.py:115
  29.4 27.6 %collective-permute-start = (bf16[64,3584]{1,0:T(8,128)(2,1)}, bf16[64,3584]{1,0:T(8,128)(2,1)S(1)}, u32[]{:S(2)}, u32[]{:S(2)}) collective-permute-start(bf16[64,3584]{1,0:T(8,128)(2,1)} %bitcast.127), channel_id=1, source_target_pairs={{0,8},{1,9},{2,10},{3,11},{4,12},{5,13},{6,14},{7,15},{8,0},{9,1},... | collective-permute-start | bytes 1376264 | tf_op jit(solution)/shard_map/ppermute | solution.py:16
  61.5 25.1 %all-to-all-start = ((bf16[16,1,20]{2,1,0:T(2,128)(2,1)}), bf16[16,1,20]{2,1,0:T(2,128)(2,1)S(1)}, u32[]{:S(2)}, u32[]{:S(2)}) async-start(bf16[16,1,20]{2,1,0:T(2,128)(2,1)} %all_to_all.20), calls=%async_computation | async-start | bytes 16384 | tf_op jit(solution)/shard_map/all_to_all | solution.py:107
  81.4 10.9 %copy-start.13 = (bf16[128,3584]{1,0:T(8,128)(2,1)S(1)}, bf16[128,3584]{1,0:T(8,128)(2,1)}, u32[]{:S(2)}) copy-start(bf16[128,3584]{1,0:T(8,128)(2,1)} %param.11) | copy-start | bytes 2752516
  86.6 85.1 %all-to-all-start.1 = ((bf16[16,20,3584]{2,1,0:T(8,128)(2,1)}), bf16[16,20,3584]{2,1,0:T(8,128)(2,1)}, u32[]{:S(2)}, u32[]{:S(2)}) async-start(bf16[16,20,3584]{2,1,0:T(8,128)(2,1)} %reshape.88), calls=%async_computation.1 | async-start | bytes 5505024 | tf_op jit(solution)/shard_map/all_to_all | solution.py:106
  171.8 79.3 %all-to-all-start.2 = ((bf16[16,20,3584]{2,1,0:T(8,128)(2,1)}), bf16[16,20,3584]{2,1,0:T(8,128)(2,1)S(1)}, u32[]{:S(2)}, u32[]{:S(2)}) async-start(bf16[16,20,3584]{2,1,0:T(8,128)(2,1)} %reshape.90), calls=%async_computation.2 | async-start | bytes 5505024 | tf_op jit(solution)/shard_map/all_to_all | solution.py:105
  176.7 333.5 %reduce-scatter.2.cloned.1.call-start = ((), (), s32[]{:S(2)}) async-start(), calls=%async_computation.7 | async-start | bytes 15597568 | tf_op jit(solution)/shard_map/reduce_scatter | solution.py:156
  253.1 7.7 %copy-start.11 = (bf16[320,3584]{1,0:T(8,128)(2,1)S(1)}, bf16[320,3584]{1,0:T(8,128)(2,1)}, u32[]{:S(2)}) copy-start(bf16[320,3584]{1,0:T(8,128)(2,1)} %reshape.89) | copy-start | bytes 6881284
  259.6 1.2 copy-start.18
  267.2 6.3 %copy-start.12 = (bf16[320,3584]{1,0:T(8,128)(2,1)S(1)}, bf16[320,3584]{1,0:T(8,128)(2,1)}, u32[]{:S(2)}) copy-start(bf16[320,3584]{1,0:T(8,128)(2,1)} %reshape.91) | copy-start | bytes 6881284
  273.5 4.3 copy-start.16
  273.5 4.3 copy-start.2
  284.3 1.1 copy-start.17
  293.2 87.3 %all-to-all-start.3 = ((bf16[16,20,3584]{2,1,0:T(8,128)(2,1)}), bf16[16,20,3584]{2,1,0:T(8,128)(2,1)S(1)}, u32[]{:S(2)}, u32[]{:S(2)}) async-start(bf16[16,20,3584]{2,1,0:T(8,128)(2,1)} %reshape.92), calls=%async_computation.3 | async-start | bytes 5505024 | tf_op jit(solution)/shard_map/all_to_all | solution.py:135
  298.2 10.1 %copy-start.7 = (f32[1,64,3584]{2,1,0:T(8,128)S(1)}, f32[1,64,3584]{2,1,0:T(8,128)}, u32[]{:S(2)}) copy-start(f32[1,64,3584]{2,1,0:T(8,128)} %param.18) | copy-start | bytes 2752516
  298.3 16.3 %copy-start.9 = (f32[1,64,3584]{2,1,0:T(8,128)S(1)}, f32[1,64,3584]{2,1,0:T(8,128)}, u32[]{:S(2)}) copy-start(f32[1,64,3584]{2,1,0:T(8,128)} %param.19) | copy-start | bytes 2752516
  300.4 211.3 %collective-permute-start.5 = (bf16[64,3584]{1,0:T(8,128)(2,1)}, bf16[64,3584]{1,0:T(8,128)(2,1)S(1)}, u32[]{:S(2)}, u32[]{:S(2)}) collective-permute-start(bf16[64,3584]{1,0:T(8,128)(2,1)} %bitcast_convert_fusion), channel_id=1, source_target_pairs={{0,8},{1,9},{2,10},{3,11},{4,12},{5,13},{6,14},{7,15},{8,0},{9,1},... | collective-permute-start | bytes 1376264 | tf_op jit(solution)/shard_map/ppermute | solution.py:16
  307.8 204.0 %collective-permute-start.4 = (bf16[64,3584]{1,0:T(8,128)(2,1)}, bf16[64,3584]{1,0:T(8,128)(2,1)}, u32[]{:S(2)}, u32[]{:S(2)}) collective-permute-start(bf16[64,3584]{1,0:T(8,128)(2,1)} %bitcast_convert_fusion.1), channel_id=1, source_target_pairs={{0,8},{1,9},{2,10},{3,11},{4,12},{5,13},{6,14},{7,15},{8,0},{9,1},... | collective-permute-start | bytes 1376264 | tf_op jit(solution)/shard_map/ppermute | solution.py:16
  309.1 202.6 %collective-permute-start.2 = (bf16[64,3584]{1,0:T(8,128)(2,1)}, bf16[64,3584]{1,0:T(8,128)(2,1)}, u32[]{:S(2)}, u32[]{:S(2)}) collective-permute-start(bf16[64,3584]{1,0:T(8,128)(2,1)} %bitcast_convert_fusion.3), channel_id=1, source_target_pairs={{0,8},{1,9},{2,10},{3,11},{4,12},{5,13},{6,14},{7,15},{8,0},{9,1},... | collective-permute-start | bytes 1376264 | tf_op jit(solution)/shard_map/ppermute | solution.py:16
  315.3 196.4 %collective-permute-start.3 = (bf16[64,3584]{1,0:T(8,128)(2,1)}, bf16[64,3584]{1,0:T(8,128)(2,1)}, u32[]{:S(2)}, u32[]{:S(2)}) collective-permute-start(bf16[64,3584]{1,0:T(8,128)(2,1)} %bitcast_convert_fusion.2), channel_id=1, source_target_pairs={{0,8},{1,9},{2,10},{3,11},{4,12},{5,13},{6,14},{7,15},{8,0},{9,1},... | collective-permute-start | bytes 1376264 | tf_op jit(solution)/shard_map/ppermute | solution.py:16
  382.6 129.1 %copy-start.3 = (bf16[64,3584]{1,0:T(8,128)(2,1)S(1)}, bf16[64,3584]{1,0:T(8,128)(2,1)}, u32[]{:S(2)}) copy-start(bf16[64,3584]{1,0:T(8,128)(2,1)} %broadcast_select_fusion) | copy-start | bytes 1376260
  382.6 129.1 %copy-start.4 = (bf16[64,3584]{1,0:T(8,128)(2,1)S(1)}, bf16[64,3584]{1,0:T(8,128)(2,1)}, u32[]{:S(2)}) copy-start(bf16[64,3584]{1,0:T(8,128)(2,1)} %broadcast_select_fusion.1) | copy-start | bytes 1376260
  382.6 129.2 %copy-start.5 = (f32[1,64,3584]{2,1,0:T(8,128)S(1)}, f32[1,64,3584]{2,1,0:T(8,128)}, u32[]{:S(2)}) copy-start(f32[1,64,3584]{2,1,0:T(8,128)} %param.21) | copy-start | bytes 2752516
  510.2 1.6 copy-start.6
  510.2 1.7 copy-start.8
  510.2 2.0 copy-start.10
  512.2 4.3 copy-start.1
Sparse Core Ops, SparseCore 0:
  29.5 93.8 all-gather.4
  125.8 108.9 all-gather.2
  284.4 225.7 reduce-scatter.1
where the time goes:
time: 524 us; the launch traced here: 523 us
  waiting for transfers between devices  366 us (70%)
  starting transfers between devices  64.4 us (12%)
  matrix products  34.1 us (7%)
  other arithmetic  23.9 us (5%)
  local copies, waits for them, and re-layouts  19.6 us (4%)
  between operations  14.7 us (3%)
    reduce_scatter x1, waiting for transfers between devices, on_device(): lax.psum_scatter(jnp.stack((up_part, down_part), axis=1).astype(jnp.bfloa...  124 us
    all_to_all x1, waiting for transfers between devices, on_device(): lax.all_to_all(send_cotan, 'expert', split_axis=0, concat_axis=0, tiled=T...  76.4 us
    all_to_all x1, waiting for transfers between devices, on_device(): lax.all_to_all(send_tokens, 'expert', split_axis=0, concat_axis=0, tiled=...  69.8 us
    all_to_all x1, waiting for transfers between devices, on_device(): lax.all_to_all(pair_grad.astype(jnp.bfloat16).reshape(experts, capacity,...  64.7 us
    ppermute x6, starting transfers between devices, partner_2(): lax.ppermute(shard, axis, [(i, i ^ 1 << stride) for i in range(lax.axis_s...  31.9 us
    ppermute x6, waiting for transfers between devices, partner_2(): lax.ppermute(shard, axis, [(i, i ^ 1 << stride) for i in range(lax.axis_s...  26 us
    all_to_all x1, starting transfers between devices, on_device(): lax.all_to_all(send_probs, 'expert', split_axis=0, concat_axis=0, tiled=T...  16.6 us
  transfers between devices with their start and end apart: 13, of which 7 were waited for; matrix products, arithmetic and copies ran while one was open for 10% of the time, Pallas kernels for 0%

commit v1 on v0

v1 whole, which is shorter than its diff:
```python
import jax
import jax.numpy as jnp
from jax import lax
from jax.sharding import Mesh
from jax.sharding import PartitionSpec as P

ADAM_STEP = 20


beta_first = 0.9
beta_second = 0.95
step_size = 0.05
adam_epsilon = 1e-08

FAR = "far"
CORE = "core"
EXPERT = "expert"


def partner_2(shard, axis, stride):
    return lax.ppermute(shard, axis, [(i, i ^ 1 << stride) for i in range(lax.axis_size(axis))])


def adam_update(weight, first, second, gradient):
    first_new = beta_first * first + (1.0 - beta_first) * gradient
    second_new = beta_second * second + (1.0 - beta_second) * gradient * gradient
    corr_first = 1.0 - beta_first**ADAM_STEP
    corr_second = 1.0 - beta_second**ADAM_STEP
    stepped = weight.astype(jnp.float32) - step_size * (first_new / corr_first) / (
        jnp.sqrt(second_new / corr_second) + adam_epsilon
    )
    return (stepped.astype(jnp.bfloat16), first_new, second_new)


def on_device(
    tokens,
    out_grad,
    routes,
    probs,
    swap_flags,
    up_weight,
    down_weight,
    up_first,
    up_second,
    down_first,
    down_second,
):
    model_width = tokens.shape[1]
    tok_rows, top_count = routes.shape
    experts = lax.axis_size(EXPERT)
    far = lax.axis_size(FAR)
    half_axis = experts // 2
    swap_bit = half_axis.bit_length() - 1
    capacity = max(2, tok_rows * top_count * 5 // (4 * experts))
    buffer_rows = experts * capacity
    local_hidden = up_weight.shape[1]
    hidden_units = local_hidden * far * lax.axis_size(CORE)
    inv_model = model_width ** (-0.5)
    inv_hidden = hidden_units ** (-0.5)
    contract_last = (((1,), (1,)), ((), ()))
    contract_first = (((0,), (0,)), ((), ()))
    my_index = lax.axis_index(EXPERT)
    expert_ids = jnp.arange(experts, dtype=jnp.int32)
    flag_mine = jnp.sum(jnp.where(expert_ids == my_index, swap_flags, 0))
    new_slot = jnp.where(swap_flags == 1, jnp.bitwise_xor(expert_ids, half_axis), expert_ids)
    swapped = flag_mine == 1

    weights = jnp.concatenate((up_weight[0], down_weight[0]), axis=0)
    weights = jnp.where(swapped, partner_2(weights, EXPERT, swap_bit), weights)
    gathered = lax.all_gather(weights, FAR, axis=0)
    up_half = gathered[:, :local_hidden].reshape(far * local_hidden, model_width)
    down_half = gathered[:, local_hidden:].reshape(far * local_hidden, model_width)

    destination = jnp.sum(
        jnp.where(routes[:, :, None] == expert_ids[None, None, :], new_slot[None, None, :], 0),
        axis=2,
    )
    pair_dest = destination.reshape(-1)
    dest_onehot = (pair_dest[:, None] == expert_ids[None, :]).astype(jnp.int32)
    earlier = jnp.cumsum(dest_onehot, axis=0) - dest_onehot
    position = jnp.sum(earlier * dest_onehot, axis=1)
    buffer_index = pair_dest * capacity + position
    buffer_ids = jnp.arange(buffer_rows, dtype=jnp.int32)
    pair_select = (buffer_ids[:, None] == buffer_index[None, :]).astype(jnp.bfloat16)
    token_select = jnp.sum(pair_select.reshape(buffer_rows, tok_rows, top_count), axis=2)
    prob_select = jnp.sum(
        (pair_select * probs.reshape(1, -1)).reshape(buffer_rows, tok_rows, top_count), axis=2
    )
    send_tokens = jnp.dot(token_select, tokens, preferred_element_type=jnp.float32)
    send_scaled = jnp.dot(prob_select, out_grad, preferred_element_type=jnp.float32)
    send = jnp.concatenate(
        (
            send_tokens.astype(jnp.bfloat16).reshape(experts, capacity, model_width),
            send_scaled.astype(jnp.bfloat16).reshape(experts, capacity, model_width),
        ),
        axis=1,
    )
    got = lax.all_to_all(send, EXPERT, split_axis=0, concat_axis=0, tiled=True)
    other = partner_2(got, CORE, 0)

    def split(block):
        return (
            block[:, :capacity].reshape(buffer_rows, model_width),
            block[:, capacity:].reshape(buffer_rows, model_width),
        )

    def hidden(rows, scaled):
        pre_act = (
            lax.dot_general(rows, up_half, contract_last, preferred_element_type=jnp.float32)
            * inv_model
        )
        back_proj = lax.dot_general(
            scaled, down_half, contract_last, preferred_element_type=jnp.float32
        )
        sigmoid_act = jax.nn.sigmoid(pre_act)
        activ = (pre_act * sigmoid_act).astype(jnp.bfloat16)
        delta = (
            back_proj * inv_hidden * sigmoid_act * (1.0 + pre_act * (1.0 - sigmoid_act))
        ).astype(jnp.bfloat16)
        return activ, delta

    rows_mine, scaled_mine = split(got)
    rows_other, scaled_other = split(other)
    activ_mine, delta_mine = hidden(rows_mine, scaled_mine)
    activ_other, delta_other = hidden(rows_other, scaled_other)
    for_other = (
        jnp.dot(delta_other, up_half, preferred_element_type=jnp.float32) * inv_model
    ).astype(jnp.bfloat16)
    from_other = partner_2(for_other, CORE, 0)
    pair_grad = (
        jnp.dot(delta_mine, up_half, preferred_element_type=jnp.float32) * inv_model
        + from_other.astype(jnp.float32)
    ).astype(jnp.bfloat16)
    half_width = model_width // 2
    returned = lax.all_to_all(
        jnp.concatenate(
            (
                pair_grad[:, :half_width].reshape(experts, capacity, half_width),
                pair_grad[:, half_width:].reshape(experts, capacity, half_width),
            ),
            axis=1,
        ),
        EXPERT,
        split_axis=0,
        concat_axis=0,
        tiled=True,
    )
    token_grad = jnp.concatenate(
        [
            lax.dot_general(
                token_select,
                part.reshape(buffer_rows, half_width),
                contract_first,
                preferred_element_type=jnp.float32,
            ).astype(jnp.bfloat16)
            for part in (returned[:, :capacity], returned[:, capacity:])
        ],
        axis=1,
    )

    def weight_grad(left_mine, right_mine, left_other, right_other, scale):
        total = lax.dot_general(
            left_mine, right_mine, contract_first, preferred_element_type=jnp.float32
        ) + lax.dot_general(
            left_other, right_other, contract_first, preferred_element_type=jnp.float32
        )
        return (total * scale).astype(jnp.bfloat16).reshape(far, local_hidden, model_width)

    up_part = weight_grad(delta_mine, rows_mine, delta_other, rows_other, inv_model)
    down_part = weight_grad(activ_mine, scaled_mine, activ_other, scaled_other, inv_hidden)
    summed = lax.psum_scatter(
        jnp.concatenate((up_part, down_part), axis=1),
        FAR,
        scatter_dimension=0,
        tiled=False,
    ).astype(jnp.float32)

    def moment(array):
        partner = partner_2(array[0].astype(jnp.bfloat16), EXPERT, swap_bit)
        return jnp.where(swapped, partner.astype(jnp.float32), array[0])

    new_up, up_first_new, up_second_new = adam_update(
        weights[:local_hidden], moment(up_first), moment(up_second), summed[:local_hidden]
    )
    new_down, down_first_new, down_second_new = adam_update(
        weights[local_hidden:], moment(down_first), moment(down_second), summed[local_hidden:]
    )
    return (
        token_grad,
        new_up[None],
        new_down[None],
        up_first_new[None],
        up_second_new[None],
        down_first_new[None],
        down_second_new[None],
    )


def solution(mesh):
    dp, expert = (mesh.shape[name] for name in ("dp", "expert"))
    fine = Mesh(mesh.devices.reshape(dp // 2, 2, expert), (FAR, CORE, EXPERT))
    rows = P((FAR, CORE, EXPERT), None)
    slots = P(EXPERT, (FAR, CORE), None)
    return jax.shard_map(
        on_device,
        mesh=fine,
        in_specs=(rows, rows, rows, rows, P()) + (slots,) * 6,
        out_specs=(rows,) + (slots,) * 6,
        check_vma=False,
    )
```

time: 524 us -> 479 us (0.914)
  waiting for transfers between devices: 366 us -> 326 us
  starting transfers between devices: 64.4 us -> 30.6 us
  local copies, waits for them, and re-layouts: 19.6 us -> 46.6 us
  other arithmetic: 23.9 us -> 33.4 us
  matrix products: 34.1 us -> 25.2 us
    reduce_scatter x1, waiting for transfers between devices: 124 us -> 79.3 us  [on_device(): lax.psum_scatter(jnp.concatenate((up_part, down_part), axis=1), FAR, scat...]
    all_to_all x4 -> x2, starting transfers between devices: 32.3 us -> 11.3 us  [the longest x1 5.98 us: on_device(): got = lax.all_to_all(send, EXPERT, split_axis=0, concat_axis=0, tiled=True)]
    all_to_all x4 -> x2, waiting for transfers between devices: 216 us -> 196 us  [the longest x1 132 us: on_device(): got = lax.all_to_all(send, EXPERT, split_axis=0, concat_axis=0, tiled=True)]
    slice x1 -> x6, local copies, waits for them, and re-layouts: 0.18 us -> 18.6 us  [the longest x2 11.4 us: split(): block[:, :capacity].reshape(buffer_rows, model_width)]
    concatenate x0 -> x5, other arithmetic: none -> 17.8 us  [the longest x1 5.67 us: on_device(): jnp.concatenate((up_part, down_part), axis=1)]
    ppermute x6 -> x7, waiting for transfers between devices: 26 us -> 40 us  [partner_2(): lax.ppermute(shard, axis, [(i, i ^ 1 << stride) for i in range(lax.axis_s...]
    ppermute x6 -> x7, starting transfers between devices: 31.9 us -> 19.2 us  [partner_2(): lax.ppermute(shard, axis, [(i, i ^ 1 << stride) for i in range(lax.axis_s...]
    all_gather x2 -> x1, waiting for transfers between devices: 0.01 us -> 10.8 us  [on_device(): gathered = lax.all_gather(weights, FAR, axis=0)]
  transfers between devices with their start and end apart: 13 -> 11, of which waited for: 7 -> 7; matrix products, arithmetic and copies ran while one was open for 10% -> 15% of each run, Pallas kernels for 0% -> 0%
where the time goes in v1:
time: 479 us; the launch traced here: 477 us
  waiting for transfers between devices  326 us (68%)
  local copies, waits for them, and re-layouts  46.6 us (10%)
  other arithmetic  33.4 us (7%)
  starting transfers between devices  30.6 us (6%)
  matrix products  25.2 us (5%)
  between operations  15 us (3%)
    all_to_all x1, waiting for transfers between devices, on_device(): got = lax.all_to_all(send, EXPERT, split_axis=0, concat_axis=0, tiled=True)  132 us
    reduce_scatter x1, waiting for transfers between devices, on_device(): lax.psum_scatter(jnp.concatenate((up_part, down_part), axis=1), FAR, scat...  79.3 us
    all_to_all x1, waiting for transfers between devices, on_device(): lax.all_to_all(jnp.concatenate((pair_grad[:, :half_width].reshape(experts...  64.2 us
    ppermute x7, waiting for transfers between devices, partner_2(): lax.ppermute(shard, axis, [(i, i ^ 1 << stride) for i in range(lax.axis_s...  40 us
    ppermute x7, starting transfers between devices, partner_2(): lax.ppermute(shard, axis, [(i, i ^ 1 << stride) for i in range(lax.axis_s...  19.2 us
    slice x2, local copies, waits for them, and re-layouts, split(): block[:, :capacity].reshape(buffer_rows, model_width)  11.4 us
    all_gather x1, waiting for transfers between devices, on_device(): gathered = lax.all_gather(weights, FAR, axis=0)  10.8 us
  transfers between devices with their start and end apart: 11, of which 7 were waited for; matrix products, arithmetic and copies ran while one was open for 15% of the time, Pallas kernels for 0%

profile of v1, /device:TPU:8, one launch (start us, length us, event | category | flops | bytes accessed | tf_op | source)
XLA Modules:
  0.0 477.0 jit_solution(6292551597779824310)
XLA Ops:
  7.2 2.2 pad_maximum_fusion.3
  9.4 7.2 %collective-permute-start = (bf16[128,3584]{1,0:T(8,128)(2,1)}, bf16[128,3584]{1,0:T(8,128)(2,1)}, u32[]{:S(2)}, u32[]{:S(2)}) collective-permute-start(bf16[128,3584]{1,0:T(8,128)(2,1)} %pad_maximum_fusion.3), channel_id=1, source_target_pairs={{0,8},{1,9},{2,10},{3,11},{4,12},{5,13},{6,14},{7,15},{8,0},{9,1},... | collective-permute-start | bytes 2752520 | tf_op jit(solution)/shard_map/ppermute | solution.py:21
  21.7 2.2 reshape.114
  24.7 2.3 reshape.113
  26.9 5.6 %pad_maximum_fusion.1 = bf16[16,40,3584]{2,1,0:T(8,128)(2,1)} fusion(bf16[16,20,3584]{2,1,0:T(8,128)(2,1)} %reshape.114, bf16[16,20,3584]{2,1,0:T(8,128)(2,1)} %reshape.113), kind=kLoop, calls=%fused_computation.8 | loop fusion | flops 9175040 | bytes 9175040 | tf_op jit(solution)/shard_map/concatenate | solution.py:91
  32.5 6.0 %all-to-all-start = ((bf16[16,40,3584]{2,1,0:T(8,128)(2,1)}), bf16[16,40,3584]{2,1,0:T(8,128)(2,1)}, u32[]{:S(2)}, u32[]{:S(2)}) async-start(bf16[16,40,3584]{2,1,0:T(8,128)(2,1)} %pad_maximum_fusion.1), calls=%async_computation | async-start | bytes 9175040 | tf_op jit(solution)/shard_map/all_to_all | solution.py:98
  39.2 17.8 %collective-permute-done = bf16[128,3584]{1,0:T(8,128)(2,1)} collective-permute-done((bf16[128,3584]{1,0:T(8,128)(2,1)}, bf16[128,3584]{1,0:T(8,128)(2,1)}, u32[]{:S(2)}, u32[]{:S(2)}) %collective-permute-start) | collective-permute-done | bytes 917536 | tf_op jit(solution)/shard_map/ppermute | solution.py:21
  58.2 131.9 %all-to-all-done = bf16[16,40,3584]{2,1,0:T(8,128)(2,1)} async-done(((bf16[16,40,3584]{2,1,0:T(8,128)(2,1)}), bf16[16,40,3584]{2,1,0:T(8,128)(2,1)}, u32[]{:S(2)}, u32[]{:S(2)}) %all-to-all-start) | async-done | bytes 4587552 | tf_op jit(solution)/shard_map/all_to_all | solution.py:98
  190.1 5.7 %fusion.36 = (bf16[16,20,3584]{2,1,0:T(8,128)(2,1)}, bf16[16,20,3584]{2,1,0:T(8,128)(2,1)}) fusion(bf16[16,40,3584]{2,1,0:T(8,128)(2,1)} %all-to-all-done), kind=kLoop, calls=%fused_computation.84 | loop fusion | bytes 9175040 | tf_op jit(solution)/shard_map/slice | solution.py:103
  195.8 4.2 reshape.115
  199.9 4.1 reshape.117
  204.1 5.7 %fusion.37 = (bf16[16,20,3584]{2,1,0:T(8,128)(2,1)}, bf16[16,20,3584]{2,1,0:T(8,128)(2,1)}) fusion(bf16[16,40,3584]{2,1,0:T(8,128)(2,1)} %collective-permute-done.1), kind=kLoop, calls=%fused_computation.85 | loop fusion | bytes 9175040 | tf_op jit(solution)/shard_map/slice | solution.py:103
  209.8 4.2 reshape.119
  213.9 2.9 reshape.120
  216.9 10.8 %all-gather.3.cloned.1.call-done = bf16[1024,3584]{1,0:T(8,128)(2,1)} async-done(((bf16[128,3584]{1,0:T(8,128)(2,1)}), bf16[1024,3584]{1,0:T(8,128)(2,1)}) %all-gather.3.cloned.1.call-update) | async-done | bytes 7340048 | tf_op jit(solution)/shard_map/all_gather | solution.py:70
  227.6 3.8 fusion.35
  236.1 2.1 fusion.17
  241.4 2.3 multiply_convert_fusion
  243.7 2.1 fusion.40
  245.9 4.2 multiply_convert_fusion.1
  250.0 5.7 %pad_maximum_fusion = bf16[8,128,3584]{2,1,0:T(8,128)(2,1)} fusion(bf16[8,64,3584]{2,1,0:T(8,128)(2,1)S(1)} %bitcast.136, bf16[8,64,3584]{2,1,0:T(8,128)(2,1)} %bitcast.137), kind=kLoop, calls=%fused_computation | loop fusion | flops 14680064 | bytes 14680064 | tf_op jit(solution)/shard_map/concatenate | solution.py:172
  255.7 3.6 fusion
  259.5 4.4 collective-permute-done.2
  269.1 3.3 pad_maximum_fusion.2
  272.4 5.3 %all-to-all-start.1 = ((bf16[16,40,1792]{2,1,0:T(8,128)(2,1)}), bf16[16,40,1792]{2,1,0:T(8,128)(2,1)S(1)}, u32[]{:S(2)}, u32[]{:S(2)}) async-start(bf16[16,40,1792]{2,1,0:T(8,128)(2,1)} %pad_maximum_fusion.2), calls=%async_computation.1 | async-start | bytes 4587520 | tf_op jit(solution)/shard_map/all_to_all | solution.py:135
  278.5 5.4 %collective-permute-start.4 = (bf16[64,3584]{1,0:T(8,128)(2,1)}, bf16[64,3584]{1,0:T(8,128)(2,1)}, u32[]{:S(2)}, u32[]{:S(2)}) collective-permute-start(bf16[64,3584]{1,0:T(8,128)(2,1)} %bitcast_convert_fusion.2), channel_id=1, source_target_pairs={{0,8},{1,9},{2,10},{3,11},{4,12},{5,13},{6,14},{7,15},{8,0},{9,1},... | collective-permute-start | bytes 1376264 | tf_op jit(solution)/shard_map/ppermute | solution.py:21
  283.9 2.0 bitcast_convert_fusion.3
  287.3 5.3 %collective-permute-start.5 = (bf16[64,3584]{1,0:T(8,128)(2,1)}, bf16[64,3584]{1,0:T(8,128)(2,1)}, u32[]{:S(2)}, u32[]{:S(2)}) collective-permute-start(bf16[64,3584]{1,0:T(8,128)(2,1)} %bitcast_convert_fusion.1), channel_id=1, source_target_pairs={{0,8},{1,9},{2,10},{3,11},{4,12},{5,13},{6,14},{7,15},{8,0},{9,1},... | collective-permute-start | bytes 1376264 | tf_op jit(solution)/shard_map/ppermute | solution.py:21
  294.0 64.2 %all-to-all-done.1 = bf16[16,40,1792]{2,1,0:T(8,128)(2,1)S(1)} async-done(((bf16[16,40,1792]{2,1,0:T(8,128)(2,1)}), bf16[16,40,1792]{2,1,0:T(8,128)(2,1)S(1)}, u32[]{:S(2)}, u32[]{:S(2)}) %all-to-all-start.1) | async-done | bytes 2293792 | tf_op jit(solution)/shard_map/all_to_all | solution.py:135
  366.4 79.3 %reduce-scatter.2.cloned.1.call-done = bf16[1,128,3584]{2,1,0:T(8,128)(2,1)} async-done(((bf16[8,128,3584]{2,1,0:T(8,128)(2,1)}), bf16[1,128,3584]{2,1,0:T(8,128)(2,1)}) %reduce-scatter.2.cloned.1.call-update) | async-done | bytes 917520 | tf_op jit(solution)/shard_map/reduce_scatter | solution.py:171
  447.0 17.9 %collective-permute-done.6 = bf16[64,3584]{1,0:T(8,128)(2,1)} collective-permute-done((bf16[64,3584]{1,0:T(8,128)(2,1)}, bf16[64,3584]{1,0:T(8,128)(2,1)}, u32[]{:S(2)}, u32[]{:S(2)}) %collective-permute-start.6) | collective-permute-done | bytes 458784 | tf_op jit(solution)/shard_map/ppermute | solution.py:21
  464.9 5.2 %fusion.34 = (f32[1,64,3584]{2,1,0:T(8,128)}, bf16[1,64,3584]{2,1,0:T(8,128)(2,1)}, f32[1,64,3584]{2,1,0:T(8,128)}, f32[1,64,3584]{2,1,0:T(8,128)}, bf16[1,64,3584]{2,1,0:T(8,128)(2,1)}, /*index=5*/f32[1,64,3584]{2,1,0:T(8,128)}) fusion(f32[1,128,3584]{2,1,0:T(8,128)S(1)} %convert_element_type.113, f32[1,64,3584]{2,1,0:T(8,128)S(1)} %copy-done.10, ...), kind=kLoop, calls=%fused_computation.82 | loop fusion | flops 8257536 | bytes 12845057 | tf_op jit(solution)/shard_map/broadcast_in_dim | solution.py:193
  (88 shorter events, 33.3 us)
Async XLA Ops:
  7.2 13.8 %copy-start = (bf16[128,3584]{1,0:T(8,128)(2,1)S(1)}, bf16[128,3584]{1,0:T(8,128)(2,1)}, u32[]{:S(2)}) copy-start(bf16[128,3584]{1,0:T(8,128)(2,1)} %param.12) | copy-start | bytes 2752516
  9.4 47.6 %collective-permute-start = (bf16[128,3584]{1,0:T(8,128)(2,1)}, bf16[128,3584]{1,0:T(8,128)(2,1)}, u32[]{:S(2)}, u32[]{:S(2)}) collective-permute-start(bf16[128,3584]{1,0:T(8,128)(2,1)} %pad_maximum_fusion.3), channel_id=1, source_target_pairs={{0,8},{1,9},{2,10},{3,11},{4,12},{5,13},{6,14},{7,15},{8,0},{9,1},... | collective-permute-start | bytes 2752520 | tf_op jit(solution)/shard_map/ppermute | solution.py:21
  21.7 2.2 copy-start.17
  32.5 24.4 %copy-start.15 = (bf16[1,64,3584]{2,1,0:T(8,128)(2,1)S(1)}, bf16[1,64,3584]{2,1,0:T(8,128)(2,1)}, u32[]{:S(2)}) copy-start(bf16[1,64,3584]{2,1,0:T(8,128)(2,1)} %param.17) | copy-start | bytes 1376260
  32.5 24.4 %copy-start.16 = (bf16[1,64,3584]{2,1,0:T(8,128)(2,1)S(1)}, bf16[1,64,3584]{2,1,0:T(8,128)(2,1)}, u32[]{:S(2)}) copy-start(bf16[1,64,3584]{2,1,0:T(8,128)(2,1)} %param.16) | copy-start | bytes 1376260
  32.5 157.6 %all-to-all-start = ((bf16[16,40,3584]{2,1,0:T(8,128)(2,1)}), bf16[16,40,3584]{2,1,0:T(8,128)(2,1)}, u32[]{:S(2)}, u32[]{:S(2)}) async-start(bf16[16,40,3584]{2,1,0:T(8,128)(2,1)} %pad_maximum_fusion.1), calls=%async_computation | async-start | bytes 9175040 | tf_op jit(solution)/shard_map/all_to_all | solution.py:98
  38.5 189.1 %all-gather.3.cloned.1.call-start = ((), (), s32[]{:S(2)}) async-start(), calls=%async_computation.4 | async-start | bytes 8257536 | tf_op jit(solution)/shard_map/all_gather | solution.py:70
  58.1 387.5 %reduce-scatter.2.cloned.1.call-start = ((), (), s32[]{:S(2)}) async-start(), calls=%async_computation.3 | async-start | bytes 8257536 | tf_op jit(solution)/shard_map/reduce_scatter | solution.py:171
  190.1 14.0 %collective-permute-start.1 = (bf16[16,40,3584]{2,1,0:T(8,128)(2,1)}, bf16[16,40,3584]{2,1,0:T(8,128)(2,1)}, u32[]{:S(2)}, u32[]{:S(2)}) collective-permute-start(bf16[16,40,3584]{2,1,0:T(8,128)(2,1)} %all-to-all-done), channel_id=1, source_target_pairs={{0,16},{16,0},{1,17},{17,1},{2,18},{18,2},{3,19},{19,3},{4,20},{20... | collective-permute-start | bytes 13762568 | tf_op jit(solution)/shard_map/ppermute | solution.py:21
  216.9 14.6 %copy-start.2 = (bf16[320,3584]{1,0:T(8,128)(2,1)}, bf16[320,3584]{1,0:T(8,128)(2,1)S(1)}, u32[]{:S(2)}) copy-start(bf16[320,3584]{1,0:T(8,128)(2,1)S(1)} %reshape.120) | copy-start | bytes 6881284
  231.5 1.9 copy-start.13
  231.5 3.0 copy-start.5
  234.5 1.6 copy-start.6
  238.3 1.6 copy-start.4
  239.9 3.8 copy-start.18
  243.7 2.1 copy-start.3
  255.7 8.1 %copy-start.14 = (bf16[8,64,3584]{2,1,0:T(8,128)(2,1)S(1)}, bf16[8,64,3584]{2,1,0:T(8,128)(2,1)}, u32[]{:S(2)}) copy-start(bf16[8,64,3584]{2,1,0:T(8,128)(2,1)} %copy-done.13) | copy-start | bytes 11010052
  255.7 8.1 %copy-start.19 = (bf16[320,512]{1,0:T(8,128)(2,1)S(1)}, bf16[320,512]{1,0:T(8,128)(2,1)}, u32[]{:S(2)}) copy-start(bf16[320,512]{1,0:T(8,128)(2,1)} %copy-done.18) | copy-start | bytes 983044
  259.3 4.5 collective-permute-start.2
  272.4 5.3 %copy-start.9 = (f32[1,64,3584]{2,1,0:T(8,128)S(1)}, f32[1,64,3584]{2,1,0:T(8,128)}, u32[]{:S(2)}) copy-start(f32[1,64,3584]{2,1,0:T(8,128)} %param.19) | copy-start | bytes 2752516
  272.4 85.8 %all-to-all-start.1 = ((bf16[16,40,1792]{2,1,0:T(8,128)(2,1)}), bf16[16,40,1792]{2,1,0:T(8,128)(2,1)S(1)}, u32[]{:S(2)}, u32[]{:S(2)}) async-start(bf16[16,40,1792]{2,1,0:T(8,128)(2,1)} %pad_maximum_fusion.2), calls=%async_computation.1 | async-start | bytes 4587520 | tf_op jit(solution)/shard_map/all_to_all | solution.py:135
  277.7 8.8 %copy-start.11 = (f32[1,64,3584]{2,1,0:T(8,128)S(1)}, f32[1,64,3584]{2,1,0:T(8,128)}, u32[]{:S(2)}) copy-start(f32[1,64,3584]{2,1,0:T(8,128)} %param.20) | copy-start | bytes 2752516
  277.7 14.9 %copy-start.12 = (f32[1,64,3584]{2,1,0:T(8,128)S(1)}, f32[1,64,3584]{2,1,0:T(8,128)}, u32[]{:S(2)}) copy-start(f32[1,64,3584]{2,1,0:T(8,128)} %param.21) | copy-start | bytes 2752516
  278.5 168.5 %collective-permute-start.4 = (bf16[64,3584]{1,0:T(8,128)(2,1)}, bf16[64,3584]{1,0:T(8,128)(2,1)}, u32[]{:S(2)}, u32[]{:S(2)}) collective-permute-start(bf16[64,3584]{1,0:T(8,128)(2,1)} %bitcast_convert_fusion.2), channel_id=1, source_target_pairs={{0,8},{1,9},{2,10},{3,11},{4,12},{5,13},{6,14},{7,15},{8,0},{9,1},... | collective-permute-start | bytes 1376264 | tf_op jit(solution)/shard_map/ppermute | solution.py:21
  285.9 161.1 %collective-permute-start.3 = (bf16[64,3584]{1,0:T(8,128)(2,1)}, bf16[64,3584]{1,0:T(8,128)(2,1)}, u32[]{:S(2)}, u32[]{:S(2)}) collective-permute-start(bf16[64,3584]{1,0:T(8,128)(2,1)} %bitcast_convert_fusion.3), channel_id=1, source_target_pairs={{0,8},{1,9},{2,10},{3,11},{4,12},{5,13},{6,14},{7,15},{8,0},{9,1},... | collective-permute-start | bytes 1376264 | tf_op jit(solution)/shard_map/ppermute | solution.py:21
  287.3 159.7 %collective-permute-start.5 = (bf16[64,3584]{1,0:T(8,128)(2,1)}, bf16[64,3584]{1,0:T(8,128)(2,1)}, u32[]{:S(2)}, u32[]{:S(2)}) collective-permute-start(bf16[64,3584]{1,0:T(8,128)(2,1)} %bitcast_convert_fusion.1), channel_id=1, source_target_pairs={{0,8},{1,9},{2,10},{3,11},{4,12},{5,13},{6,14},{7,15},{8,0},{9,1},... | collective-permute-start | bytes 1376264 | tf_op jit(solution)/shard_map/ppermute | solution.py:21
  293.5 171.5 %collective-permute-start.6 = (bf16[64,3584]{1,0:T(8,128)(2,1)}, bf16[64,3584]{1,0:T(8,128)(2,1)}, u32[]{:S(2)}, u32[]{:S(2)}) collective-permute-start(bf16[64,3584]{1,0:T(8,128)(2,1)} %bitcast_convert_fusion), channel_id=1, source_target_pairs={{0,8},{1,9},{2,10},{3,11},{4,12},{5,13},{6,14},{7,15},{8,0},{9,1},... | collective-permute-start | bytes 1376264 | tf_op jit(solution)/shard_map/ppermute | solution.py:21
  360.1 1.8 copy-start.8
  363.5 101.4 %copy-start.7 = (bf16[128,3584]{1,0:T(8,128)(2,1)S(1)}, bf16[128,3584]{1,0:T(8,128)(2,1)}, u32[]{:S(2)}) copy-start(bf16[128,3584]{1,0:T(8,128)(2,1)} %broadcast_select_fusion) | copy-start | bytes 2752516
  363.6 101.4 %copy-start.10 = (f32[1,64,3584]{2,1,0:T(8,128)S(1)}, f32[1,64,3584]{2,1,0:T(8,128)}, u32[]{:S(2)}) copy-start(f32[1,64,3584]{2,1,0:T(8,128)} %param.19) | copy-start | bytes 2752516
  464.9 5.2 %copy-start.1 = (bf16[128,3584]{1,0:T(8,128)(2,1)S(1)}, bf16[128,3584]{1,0:T(8,128)(2,1)}, u32[]{:S(2)}) copy-start(bf16[128,3584]{1,0:T(8,128)(2,1)} %param.12) | copy-start | bytes 2752516
Sparse Core Ops, SparseCore 0:
  58.2 169.3 all-gather.2
  255.8 189.7 reduce-scatter.1

commit v2 on v1

--- a/solution.py
+++ b/solution.py
@@ -12,7 +12,8 @@
 step_size = 0.05
 adam_epsilon = 1e-08
 
-FAR = "far"
+NEAR = "near"
+RING = "ring"
 CORE = "core"
 EXPERT = "expert"
 
@@ -48,13 +49,15 @@
     model_width = tokens.shape[1]
     tok_rows, top_count = routes.shape
     experts = lax.axis_size(EXPERT)
-    far = lax.axis_size(FAR)
+    ring = lax.axis_size(RING)
+    near = lax.axis_size(NEAR)
+    chips = ring * near
     half_axis = experts // 2
     swap_bit = half_axis.bit_length() - 1
     capacity = max(2, tok_rows * top_count * 5 // (4 * experts))
     buffer_rows = experts * capacity
     local_hidden = up_weight.shape[1]
-    hidden_units = local_hidden * far * lax.axis_size(CORE)
+    hidden_units = local_hidden * chips * lax.axis_size(CORE)
     inv_model = model_width ** (-0.5)
     inv_hidden = hidden_units ** (-0.5)
     contract_last = (((1,), (1,)), ((), ()))
@@ -67,9 +70,10 @@
 
     weights = jnp.concatenate((up_weight[0], down_weight[0]), axis=0)
     weights = jnp.where(swapped, partner_2(weights, EXPERT, swap_bit), weights)
-    gathered = lax.all_gather(weights, FAR, axis=0)
-    up_half = gathered[:, :local_hidden].reshape(far * local_hidden, model_width)
-    down_half = gathered[:, local_hidden:].reshape(far * local_hidden, model_width)
+    both = jnp.stack((weights, partner_2(weights, NEAR, 0)), axis=0)
+    gathered = lax.all_gather(both, RING, axis=0)
+    up_half = gathered[:, :, :local_hidden].reshape(chips * local_hidden, model_width)
+    down_half = gathered[:, :, local_hidden:].reshape(chips * local_hidden, model_width)
 
     destination = jnp.sum(
         jnp.where(routes[:, :, None] == expert_ids[None, None, :], new_slot[None, None, :], 0),
@@ -86,22 +90,37 @@
     prob_select = jnp.sum(
         (pair_select * probs.reshape(1, -1)).reshape(buffer_rows, tok_rows, top_count), axis=2
     )
-    send_tokens = jnp.dot(token_select, tokens, preferred_element_type=jnp.float32)
-    send_scaled = jnp.dot(prob_select, out_grad, preferred_element_type=jnp.float32)
-    send = jnp.concatenate(
+    zeros = jnp.zeros((experts, capacity, tok_rows), jnp.bfloat16)
+    mixed_select = jnp.concatenate(
         (
-            send_tokens.astype(jnp.bfloat16).reshape(experts, capacity, model_width),
-            send_scaled.astype(jnp.bfloat16).reshape(experts, capacity, model_width),
+            jnp.concatenate((token_select.reshape(zeros.shape), zeros), axis=2),
+            jnp.concatenate((zeros, prob_select.reshape(zeros.shape)), axis=2),
         ),
         axis=1,
+    ).reshape(2 * buffer_rows, 2 * tok_rows)
+    send = (
+        jnp.dot(
+            mixed_select,
+            jnp.concatenate((tokens, out_grad), axis=0),
+            preferred_element_type=jnp.float32,
+        )
+        .astype(jnp.bfloat16)
+        .reshape(experts, 2 * capacity, model_width)
     )
     got = lax.all_to_all(send, EXPERT, split_axis=0, concat_axis=0, tiled=True)
     other = partner_2(got, CORE, 0)
 
+    order = jnp.arange(buffer_rows, dtype=jnp.int32)
+    place = (order // capacity) * (2 * capacity) + order % capacity
+    mixed_ids = jnp.arange(2 * buffer_rows, dtype=jnp.int32)
+    pick_rows = (place[:, None] == mixed_ids[None, :]).astype(jnp.bfloat16)
+    pick_scaled = (place[:, None] + capacity == mixed_ids[None, :]).astype(jnp.bfloat16)
+
     def split(block):
-        return (
-            block[:, :capacity].reshape(buffer_rows, model_width),
-            block[:, capacity:].reshape(buffer_rows, model_width),
+        flat = block.reshape(2 * buffer_rows, model_width)
+        return tuple(
+            jnp.dot(pick, flat, preferred_element_type=jnp.float32).astype(jnp.bfloat16)
+            for pick in (pick_rows, pick_scaled)
         )
 
     def hidden(rows, scaled):
@@ -164,26 +183,33 @@
         ) + lax.dot_general(
             left_other, right_other, contract_first, preferred_element_type=jnp.float32
         )
-        return (total * scale).astype(jnp.bfloat16).reshape(far, local_hidden, model_width)
+        return (total * scale).astype(jnp.bfloat16).reshape(ring, near, local_hidden, model_width)
 
     up_part = weight_grad(delta_mine, rows_mine, delta_other, rows_other, inv_model)
     down_part = weight_grad(activ_mine, scaled_mine, activ_other, scaled_other, inv_hidden)
-    summed = lax.psum_scatter(
-        jnp.concatenate((up_part, down_part), axis=1),
-        FAR,
-        scatter_dimension=0,
-        tiled=False,
-    ).astype(jnp.float32)
-
-    def moment(array):
-        partner = partner_2(array[0].astype(jnp.bfloat16), EXPERT, swap_bit)
+    own, beside = lax.psum_scatter(
+        jnp.concatenate((up_part, down_part), axis=2), RING, scatter_dimension=0, tiled=False
+    )
+    summed = own.astype(jnp.float32) + partner_2(beside, NEAR, 0).astype(jnp.float32)
+    held, _ = lax.optimization_barrier(
+        (
+            tuple(
+                array[0].astype(jnp.bfloat16)
+                for array in (up_first, up_second, down_first, down_second)
+            ),
+            got,
+        )
+    )
+
+    def moment(array, rounded):
+        partner = partner_2(rounded, EXPERT, swap_bit)
         return jnp.where(swapped, partner.astype(jnp.float32), array[0])
 
     new_up, up_first_new, up_second_new = adam_update(
-        weights[:local_hidden], moment(up_first), moment(up_second), summed[:local_hidden]
+        weights[:local_hidden], moment(up_first, held[0]), moment(up_second, held[1]), summed[:local_hidden]
     )
     new_down, down_first_new, down_second_new = adam_update(
-        weights[local_hidden:], moment(down_first), moment(down_second), summed[local_hidden:]
+        weights[local_hidden:], moment(down_first, held[2]), moment(down_second, held[3]), summed[local_hidden:]
     )
     return (
         token_grad,
@@ -198,9 +224,9 @@
 
 def solution(mesh):
     dp, expert = (mesh.shape[name] for name in ("dp", "expert"))
-    fine = Mesh(mesh.devices.reshape(dp // 2, 2, expert), (FAR, CORE, EXPERT))
-    rows = P((FAR, CORE, EXPERT), None)
-    slots = P(EXPERT, (FAR, CORE), None)
+    fine = Mesh(mesh.devices.reshape(2, dp // 4, 2, expert), (NEAR, RING, CORE, EXPERT))
+    rows = P((NEAR, RING, CORE, EXPERT), None)
+    slots = P(EXPERT, (NEAR, RING, CORE), None)
     return jax.shard_map(
         on_device,
         mesh=fine,

time: 479 us -> 427 us (0.89)
  waiting for transfers between devices: 326 us -> 126 us
  blocking collectives: 0 us -> 89 us
  starting transfers between devices: 30.6 us -> 111 us
  local copies, waits for them, and re-layouts: 46.6 us -> 15.5 us
  matrix products: 25.2 us -> 42.2 us
  other arithmetic: 33.4 us -> 24.2 us
    all_to_all x1 -> x0, waiting for transfers between devices: 132 us -> none  [on_device(): got = lax.all_to_all(send, EXPERT, split_axis=0, concat_axis=0, tiled=True)]
    all_to_all x0 -> x1, blocking collectives: none -> 89 us  [on_device(): got = lax.all_to_all(send, EXPERT, split_axis=0, concat_axis=0, tiled=True)]
    reduce_scatter x1, waiting for transfers between devices: 79.3 us -> 0.01 us  [on_device(): lax.psum_scatter(jnp.concatenate((up_part, down_part), axis=2), RING, sca...]
    ppermute x7 -> x9, starting transfers between devices: 19.2 us -> 83 us  [partner_2(): lax.ppermute(shard, axis, [(i, i ^ 1 << stride) for i in range(lax.axis_s...]
    ppermute x7 -> x9, waiting for transfers between devices: 40 us -> 93 us  [partner_2(): lax.ppermute(shard, axis, [(i, i ^ 1 << stride) for i in range(lax.axis_s...]
    all_to_all x1, waiting for transfers between devices: 64.2 us -> 32.6 us  [on_device(): lax.all_to_all(jnp.concatenate((pair_grad[:, :half_width].reshape(experts...]
    all_to_all x1, starting transfers between devices: 5.28 us -> 27.8 us  [on_device(): lax.all_to_all(jnp.concatenate((pair_grad[:, :half_width].reshape(experts...]
    reshape x6 -> x2, local copies, waits for them, and re-layouts: 19.8 us -> 0.04 us  [the longest x1 0.02 us: on_device(): prob_select.reshape(zeros.shape)]
  transfers between devices with their start and end apart: 11 -> 12, of which waited for: 7 -> 5; matrix products, arithmetic and copies ran while one was open for 15% -> 12% of each run, Pallas kernels for 0% -> 0%
where the time goes in v2:
time: 427 us; the launch traced here: 423 us
  waiting for transfers between devices  126 us (30%)
  starting transfers between devices  111 us (26%)
  blocking collectives  89 us (21%)
  matrix products  42.2 us (10%)
  other arithmetic  24.2 us (6%)
  local copies, waits for them, and re-layouts  15.5 us (4%)
  between operations  15.1 us (4%)
    ppermute x9, waiting for transfers between devices, partner_2(): lax.ppermute(shard, axis, [(i, i ^ 1 << stride) for i in range(lax.axis_s...  93 us
    all_to_all x1, blocking collectives, on_device(): got = lax.all_to_all(send, EXPERT, split_axis=0, concat_axis=0, tiled=True)  89 us
    ppermute x9, starting transfers between devices, partner_2(): lax.ppermute(shard, axis, [(i, i ^ 1 << stride) for i in range(lax.axis_s...  83 us
    all_to_all x1, waiting for transfers between devices, on_device(): lax.all_to_all(jnp.concatenate((pair_grad[:, :half_width].reshape(experts...  32.6 us
    all_to_all x1, starting transfers between devices, on_device(): lax.all_to_all(jnp.concatenate((pair_grad[:, :half_width].reshape(experts...  27.8 us
    dot_general x4, matrix products, split(): jnp.dot(pick, flat, preferred_element_type=jnp.float32).astype(jnp.bfloat16)  18.5 us
  transfers between devices with their start and end apart: 12, of which 5 were waited for; matrix products, arithmetic and copies ran while one was open for 12% of the time, Pallas kernels for 0%

profile of v2, /device:TPU:8, one launch (start us, length us, event | category | flops | bytes accessed | tf_op | source)
XLA Modules:
  0.0 422.5 jit_solution(11243043033066579525)
XLA Ops:
  8.4 7.3 %collective-permute-start = (bf16[128,3584]{1,0:T(8,128)(2,1)S(1)}, bf16[128,3584]{1,0:T(8,128)(2,1)S(1)}, u32[]{:S(2)}, u32[]{:S(2)}) collective-permute-start(bf16[128,3584]{1,0:T(8,128)(2,1)S(1)} %pad_maximum_fusion.3), channel_id=1, source_target_pairs={{0,8},{1,9},{2,10},{3,11},{4,12},{5,13},{6,14},{7,15},{8,0},{9,1},... | collective-permute-start | bytes 2752520 | tf_op jit(solution)/shard_map/ppermute | solution.py:22
  17.7 36.8 %collective-permute-done = bf16[128,3584]{1,0:T(8,128)(2,1)S(1)} collective-permute-done((bf16[128,3584]{1,0:T(8,128)(2,1)S(1)}, bf16[128,3584]{1,0:T(8,128)(2,1)S(1)}, u32[]{:S(2)}, u32[]{:S(2)}) %collective-permute-start) | collective-permute-done | bytes 917536 | tf_op jit(solution)/shard_map/ppermute | solution.py:22
  55.8 2.6 collective-permute-start.1
  59.5 18.5 %collective-permute-done.1 = bf16[128,3584]{1,0:T(8,128)(2,1)S(1)} collective-permute-done((bf16[128,3584]{1,0:T(8,128)(2,1)S(1)}, bf16[128,3584]{1,0:T(8,128)(2,1)S(1)}, u32[]{:S(2)}, u32[]{:S(2)}) %collective-permute-start.1) | collective-permute-done | bytes 917536 | tf_op jit(solution)/shard_map/ppermute | solution.py:22
  78.0 1.4 pad_maximum_fusion.2
  82.3 89.0 %all_to_all.10 = bf16[16,40,3584]{2,1,0:T(8,128)(2,1)} all-to-all(bf16[16,40,3584]{2,1,0:T(8,128)(2,1)S(1)} %bitcast.124), channel_id=1, replica_groups=mesh['near'=2,'ring'=4,'core'=2,'expert'=16] {'expert'}, dimensions={0} | all-to-all | bytes 9175040 | tf_op jit(solution)/shard_map/all_to_all | solution.py:110
  171.3 4.3 %convolution_convert_fusion.4 = bf16[320,3584]{1,0:T(8,128)(2,1)S(1)} fusion(bf16[640,3584]{1,0:T(8,128)(2,1)} %bitcast.3, s32[320]{0:T(512)S(1)} %broadcast_add_fusion), kind=kOutput, calls=%fused_computation.10 | convolution fusion | flops 1469358080 | bytes 6882560 | tf_op jit(solution)/shard_map/dot_general | solution.py:122
  175.6 5.6 %convolution_convert_fusion.3 = bf16[320,3584]{1,0:T(8,128)(2,1)} fusion(bf16[640,3584]{1,0:T(8,128)(2,1)} %bitcast.3, s32[320]{0:T(512)S(1)} %fusion.43), kind=kOutput, calls=%fused_computation.9 | convolution fusion | flops 1469358080 | bytes 6882560 | tf_op jit(solution)/shard_map/dot_general | solution.py:122
  181.3 4.0 fusion.55
  186.6 1.5 fusion.8
  188.1 2.1 fusion.58
  190.3 2.2 fusion.26
  192.4 4.3 %convolution_convert_fusion.2 = bf16[320,3584]{1,0:T(8,128)(2,1)S(1)} fusion(bf16[640,3584]{1,0:T(8,128)(2,1)} %bitcast.11, s32[320]{0:T(512)S(1)} %broadcast_add_fusion), kind=kOutput, calls=%fused_computation.8 | convolution fusion | flops 1469358080 | bytes 6882560 | tf_op jit(solution)/shard_map/dot_general | solution.py:122
  196.7 4.3 %convolution_convert_fusion.1 = bf16[320,3584]{1,0:T(8,128)(2,1)S(1)} fusion(bf16[640,3584]{1,0:T(8,128)(2,1)} %bitcast.11, s32[320]{0:T(512)S(1)} %fusion.43), kind=kOutput, calls=%fused_computation.7 | convolution fusion | flops 1469358080 | bytes 6882560 | tf_op jit(solution)/shard_map/dot_general | solution.py:122
  201.0 1.6 convolution_multiply_fusion.2
  202.6 1.5 fusion.9
  204.1 2.3 multiply_convert_fusion
  206.4 4.1 multiply_convert_fusion.1
  210.5 5.5 %pad_maximum_fusion = bf16[4,2,128,3584]{3,2,1,0:T(8,128)(2,1)} fusion(bf16[4,2,64,3584]{3,2,1,0:T(8,128)(2,1)S(1)} %bitcast.122, bf16[4,2,64,3584]{3,2,1,0:T(8,128)(2,1)} %bitcast.123), kind=kLoop, calls=%fused_computation | loop fusion | flops 14680064 | bytes 14680064 | tf_op jit(solution)/shard_map/concatenate | solution.py:191
  216.0 3.6 fusion
  220.2 4.1 collective-permute-done.3
  229.4 3.3 pad_maximum_fusion.1
  232.6 27.8 %all-to-all-start.1 = ((bf16[16,40,1792]{2,1,0:T(8,128)(2,1)}), bf16[16,40,1792]{2,1,0:T(8,128)(2,1)S(1)}, u32[]{:S(2)}, u32[]{:S(2)}) async-start(bf16[16,40,1792]{2,1,0:T(8,128)(2,1)} %pad_maximum_fusion.1), calls=%async_computation.1 | async-start | bytes 4587520 | tf_op jit(solution)/shard_map/all_to_all | solution.py:154
  260.4 2.6 bitcast_convert_fusion.2
  264.1 5.3 %collective-permute-start.6 = (bf16[64,3584]{1,0:T(8,128)(2,1)}, bf16[64,3584]{1,0:T(8,128)(2,1)}, u32[]{:S(2)}, u32[]{:S(2)}) collective-permute-start(bf16[64,3584]{1,0:T(8,128)(2,1)} %get-tuple-element.12), channel_id=1, source_target_pairs={{0,8},{1,9},{2,10},{3,11},{4,12},{5,13},{6,14},{7,15},{8,0},{9,1},... | collective-permute-start | bytes 1376264 | tf_op jit(solution)/shard_map/ppermute | solution.py:22
  270.0 5.3 %collective-permute-start.7 = (bf16[64,3584]{1,0:T(8,128)(2,1)}, bf16[64,3584]{1,0:T(8,128)(2,1)}, u32[]{:S(2)}, u32[]{:S(2)}) collective-permute-start(bf16[64,3584]{1,0:T(8,128)(2,1)} %get-tuple-element.13), channel_id=1, source_target_pairs={{0,8},{1,9},{2,10},{3,11},{4,12},{5,13},{6,14},{7,15},{8,0},{9,1},... | collective-permute-start | bytes 1376264 | tf_op jit(solution)/shard_map/ppermute | solution.py:22
  276.0 32.6 %all-to-all-done.1 = bf16[16,40,1792]{2,1,0:T(8,128)(2,1)S(1)} async-done(((bf16[16,40,1792]{2,1,0:T(8,128)(2,1)}), bf16[16,40,1792]{2,1,0:T(8,128)(2,1)S(1)}, u32[]{:S(2)}, u32[]{:S(2)}) %all-to-all-start.1) | async-done | bytes 2293792 | tf_op jit(solution)/shard_map/all_to_all | solution.py:154
  308.6 2.0 fusion.56
  310.6 1.5 reshape.150
  314.9 60.6 %collective-permute-start.5 = (bf16[128,3584]{1,0:T(8,128)(2,1)S(1)}, bf16[128,3584]{1,0:T(8,128)(2,1)S(1)}, u32[]{:S(2)}, u32[]{:S(2)}) collective-permute-start(bf16[128,3584]{1,0:T(8,128)(2,1)S(1)} %slice_bitcast_fusion), channel_id=1, source_target_pairs={{0,128},{128,0},{1,129},{129,1},{2,130},{130,2},{3,131},{131,3},{4... | collective-permute-start | bytes 2752520 | tf_op jit(solution)/shard_map/ppermute | solution.py:22
  377.4 33.6 %collective-permute-done.5 = bf16[128,3584]{1,0:T(8,128)(2,1)S(1)} collective-permute-done((bf16[128,3584]{1,0:T(8,128)(2,1)S(1)}, bf16[128,3584]{1,0:T(8,128)(2,1)S(1)}, u32[]{:S(2)}, u32[]{:S(2)}) %collective-permute-start.5) | collective-permute-done | bytes 917536 | tf_op jit(solution)/shard_map/ppermute | solution.py:22
  411.4 4.4 %fusion.54 = (f32[1,64,3584]{2,1,0:T(8,128)}, bf16[1,64,3584]{2,1,0:T(8,128)(2,1)}, f32[1,64,3584]{2,1,0:T(8,128)}, f32[1,64,3584]{2,1,0:T(8,128)}, bf16[1,64,3584]{2,1,0:T(8,128)(2,1)}, /*index=5*/f32[1,64,3584]{2,1,0:T(8,128)}) fusion(f32[128,3584]{1,0:T(8,128)S(1)} %convert_add_fusion, f32[1,64,3584]{2,1,0:T(8,128)S(1)} %copy-done.4, ...), kind=kLoop, calls=%fused_computation.115 | loop fusion | flops 8257536 | bytes 12845057 | tf_op jit(solution)/shard_map/broadcast_in_dim | solution.py:219
  (86 shorter events, 21.9 us)
Async XLA Ops:
  7.2 174.1 %all-gather.3.cloned.1.call-start = ((), (), s32[]{:S(2)}) async-start(), calls=%async_computation.4 | async-start | bytes 9175040 | tf_op jit(solution)/shard_map/all_gather | solution.py:74
  7.2 51.2 %copy-start.16 = (s32[128,2]{0,1:T(2,128)S(1)}, s32[128,2]{0,1:T(2,128)}, u32[]{:S(2)}) copy-start(s32[128,2]{0,1:T(2,128)} %param.13) | copy-start | bytes 3076
  8.4 46.0 %collective-permute-start = (bf16[128,3584]{1,0:T(8,128)(2,1)S(1)}, bf16[128,3584]{1,0:T(8,128)(2,1)S(1)}, u32[]{:S(2)}, u32[]{:S(2)}) collective-permute-start(bf16[128,3584]{1,0:T(8,128)(2,1)S(1)} %pad_maximum_fusion.3), channel_id=1, source_target_pairs={{0,8},{1,9},{2,10},{3,11},{4,12},{5,13},{6,14},{7,15},{8,0},{9,1},... | collective-permute-start | bytes 2752520 | tf_op jit(solution)/shard_map/ppermute | solution.py:22
  55.8 22.2 %collective-permute-start.1 = (bf16[128,3584]{1,0:T(8,128)(2,1)S(1)}, bf16[128,3584]{1,0:T(8,128)(2,1)S(1)}, u32[]{:S(2)}, u32[]{:S(2)}) collective-permute-start(bf16[128,3584]{1,0:T(8,128)(2,1)S(1)} %broadcast_select_fusion), channel_id=1, source_target_pairs={{0,128},{128,0},{1,129},{129,1},{2,130},{130,2},{3,131},{131,3},{4... | collective-permute-start | bytes 2752520 | tf_op jit(solution)/shard_map/ppermute | solution.py:22
  78.0 2.1 copy-start.17
  79.5 1.2 copy-start.12
  79.5 1.5 copy-start.13
  79.5 234.0 %reduce-scatter.2.cloned.1.call-start = ((), (), s32[]{:S(2)}) async-start(), calls=%async_computation.3 | async-start | bytes 9175040 | tf_op jit(solution)/shard_map/reduce_scatter | solution.py:190
  171.3 21.1 %collective-permute-start.2 = (bf16[16,40,3584]{2,1,0:T(8,128)(2,1)}, bf16[16,40,3584]{2,1,0:T(8,128)(2,1)}, u32[]{:S(2)}, u32[]{:S(2)}) collective-permute-start(bf16[16,40,3584]{2,1,0:T(8,128)(2,1)} %all_to_all.10), channel_id=1, source_target_pairs={{0,16},{16,0},{1,17},{17,1},{2,18},{18,2},{3,19},{19,3},{4,20},{20... | collective-permute-start | bytes 13762568 | tf_op jit(solution)/shard_map/ppermute | solution.py:22
  181.3 4.0 copy-start.10
  185.2 15.8 %copy-start.2 = (bf16[4,2,64,3584]{3,2,1,0:T(8,128)(2,1)}, bf16[4,2,64,3584]{3,2,1,0:T(8,128)(2,1)S(1)}, u32[]{:S(2)}) copy-start(bf16[4,2,64,3584]{3,2,1,0:T(8,128)(2,1)S(1)} %get-tuple-element.17) | copy-start | bytes 11010052
  188.1 2.1 copy-start.14
  216.0 8.3 %copy-start.3 = (bf16[4,2,64,3584]{3,2,1,0:T(8,128)(2,1)S(1)}, bf16[4,2,64,3584]{3,2,1,0:T(8,128)(2,1)}, u32[]{:S(2)}) copy-start(bf16[4,2,64,3584]{3,2,1,0:T(8,128)(2,1)} %copy-done.2) | copy-start | bytes 11010052
  216.0 8.3 %copy-start.15 = (bf16[320,512]{1,0:T(8,128)(2,1)S(1)}, bf16[320,512]{1,0:T(8,128)(2,1)}, u32[]{:S(2)}) copy-start(bf16[320,512]{1,0:T(8,128)(2,1)} %copy-done.14) | copy-start | bytes 983044
  219.6 4.7 %collective-permute-start.3 = (bf16[320,3584]{1,0:T(8,128)(2,1)S(1)}, bf16[320,3584]{1,0:T(8,128)(2,1)S(1)}, u32[]{:S(2)}, u32[]{:S(2)}) collective-permute-start(bf16[320,3584]{1,0:T(8,128)(2,1)S(1)} %fusion), channel_id=1, source_target_pairs={{0,16},{16,0},{1,17},{17,1},{2,18},{18,2},{3,19},{19,3},{4,20},{20... | collective-permute-start | bytes 6881288 | tf_op jit(solution)/shard_map/ppermute | solution.py:22
  232.6 76.0 %all-to-all-start.1 = ((bf16[16,40,1792]{2,1,0:T(8,128)(2,1)}), bf16[16,40,1792]{2,1,0:T(8,128)(2,1)S(1)}, u32[]{:S(2)}, u32[]{:S(2)}) async-start(bf16[16,40,1792]{2,1,0:T(8,128)(2,1)} %pad_maximum_fusion.1), calls=%async_computation.1 | async-start | bytes 4587520 | tf_op jit(solution)/shard_map/all_to_all | solution.py:154
  260.4 2.7 copy-start.6
  260.4 2.6 copy-start.8
  264.1 147.2 %collective-permute-start.6 = (bf16[64,3584]{1,0:T(8,128)(2,1)}, bf16[64,3584]{1,0:T(8,128)(2,1)}, u32[]{:S(2)}, u32[]{:S(2)}) collective-permute-start(bf16[64,3584]{1,0:T(8,128)(2,1)} %get-tuple-element.12), channel_id=1, source_target_pairs={{0,8},{1,9},{2,10},{3,11},{4,12},{5,13},{6,14},{7,15},{8,0},{9,1},... | collective-permute-start | bytes 1376264 | tf_op jit(solution)/shard_map/ppermute | solution.py:22
  269.4 141.8 %collective-permute-start.4 = (bf16[64,3584]{1,0:T(8,128)(2,1)}, bf16[64,3584]{1,0:T(8,128)(2,1)}, u32[]{:S(2)}, u32[]{:S(2)}) collective-permute-start(bf16[64,3584]{1,0:T(8,128)(2,1)} %get-tuple-element.11), channel_id=1, source_target_pairs={{0,8},{1,9},{2,10},{3,11},{4,12},{5,13},{6,14},{7,15},{8,0},{9,1},... | collective-permute-start | bytes 1376264 | tf_op jit(solution)/shard_map/ppermute | solution.py:22
  270.0 141.3 %collective-permute-start.7 = (bf16[64,3584]{1,0:T(8,128)(2,1)}, bf16[64,3584]{1,0:T(8,128)(2,1)}, u32[]{:S(2)}, u32[]{:S(2)}) collective-permute-start(bf16[64,3584]{1,0:T(8,128)(2,1)} %get-tuple-element.13), channel_id=1, source_target_pairs={{0,8},{1,9},{2,10},{3,11},{4,12},{5,13},{6,14},{7,15},{8,0},{9,1},... | collective-permute-start | bytes 1376264 | tf_op jit(solution)/shard_map/ppermute | solution.py:22
  275.4 135.9 %collective-permute-start.8 = (bf16[64,3584]{1,0:T(8,128)(2,1)}, bf16[64,3584]{1,0:T(8,128)(2,1)}, u32[]{:S(2)}, u32[]{:S(2)}) collective-permute-start(bf16[64,3584]{1,0:T(8,128)(2,1)} %get-tuple-element.14), channel_id=1, source_target_pairs={{0,8},{1,9},{2,10},{3,11},{4,12},{5,13},{6,14},{7,15},{8,0},{9,1},... | collective-permute-start | bytes 1376264 | tf_op jit(solution)/shard_map/ppermute | solution.py:22
  310.6 1.8 copy-start
  313.5 62.4 %copy-start.1 = (bf16[320,1792]{1,0:T(8,128)(2,1)S(1)}, bf16[320,1792]{1,0:T(8,128)(2,1)}, u32[]{:S(2)}) copy-start(bf16[320,1792]{1,0:T(8,128)(2,1)} %reshape.149) | copy-start | bytes 3440644
  314.8 96.2 %copy-start.11 = (bf16[1,2,128,3584]{3,2,1,0:T(8,128)(2,1)S(1)}, bf16[1,2,128,3584]{3,2,1,0:T(8,128)(2,1)}, u32[]{:S(2)}) copy-start(bf16[1,2,128,3584]{3,2,1,0:T(8,128)(2,1)} %reduce-scatter.2.cloned.1.call-done) | copy-start | bytes 5505028
  314.9 96.2 %collective-permute-start.5 = (bf16[128,3584]{1,0:T(8,128)(2,1)S(1)}, bf16[128,3584]{1,0:T(8,128)(2,1)S(1)}, u32[]{:S(2)}, u32[]{:S(2)}) collective-permute-start(bf16[128,3584]{1,0:T(8,128)(2,1)S(1)} %slice_bitcast_fusion), channel_id=1, source_target_pairs={{0,128},{128,0},{1,129},{129,1},{2,130},{130,2},{3,131},{131,3},{4... | collective-permute-start | bytes 2752520 | tf_op jit(solution)/shard_map/ppermute | solution.py:22
  376.3 35.0 %copy-start.4 = (f32[1,64,3584]{2,1,0:T(8,128)S(1)}, f32[1,64,3584]{2,1,0:T(8,128)}, u32[]{:S(2)}) copy-start(f32[1,64,3584]{2,1,0:T(8,128)} %param.19) | copy-start | bytes 2752516
  376.4 35.0 %copy-start.5 = (f32[1,64,3584]{2,1,0:T(8,128)S(1)}, f32[1,64,3584]{2,1,0:T(8,128)}, u32[]{:S(2)}) copy-start(f32[1,64,3584]{2,1,0:T(8,128)} %param.18) | copy-start | bytes 2752516
  376.4 35.0 %copy-start.7 = (f32[1,64,3584]{2,1,0:T(8,128)S(1)}, f32[1,64,3584]{2,1,0:T(8,128)}, u32[]{:S(2)}) copy-start(f32[1,64,3584]{2,1,0:T(8,128)} %param.20) | copy-start | bytes 2752516
  376.4 35.0 %copy-start.9 = (f32[1,64,3584]{2,1,0:T(8,128)S(1)}, f32[1,64,3584]{2,1,0:T(8,128)}, u32[]{:S(2)}) copy-start(f32[1,64,3584]{2,1,0:T(8,128)} %param.21) | copy-start | bytes 2752516
Sparse Core Ops, SparseCore 0:
  79.6 78.2 all-gather.2
  216.1 94.7 reduce-scatter.1
